TPU v7x, 128 devices: a whole 4x4x4 slice. The times are simulated.
128 devices in a mesh: chan: 32 (over x, z, core), rep: 4 (over y).
Axes of the slice: x: 4, y: 4, z: 4, core: 2. Of those that a mesh axis runs over, the one named last changes fastest.
Arguments:
- block_sizes: int32 [64], P('chan'), may hold values from 64 to 2048, as said below
- amplitudes: bfloat16 [64, 2048, 384], P('chan'), may hold values from -6 to 6
- ladder_coupling: bfloat16 [64, 2048, 2048], P('chan', 'rep'), may hold values from -0.125 to 0.125
- bare_coupling: bfloat16 [64, 2048, 384], P('chan', 'rep'), may hold values from -6 to 6
- particle_energy: float32 [64, 2048], P('chan', 'rep'), may hold values from 0.5 to 8
- hole_energy: float32 [64, 384], P('chan'), may hold values from -8 to -0.5
- cycle_coupling: bfloat16 [192, 2048, 2048], P('chan', None, 'rep'), may hold values from -0.125 to 0.125
- pandya_rows: int32 [192, 2048], P('chan', 'rep'), may hold values from 0 to 131071, as said below
- pandya_weight: float32 [192, 2048], P('chan', 'rep'), may hold values from -1 to 1
Outputs:
- updated: bfloat16 [64, 2048, 384], P('chan', 'rep')
Inputs may be any that keep to these rules, and one draw needn't show every extreme that they name: `block_sizes`: some channel has exactly 2048 valid rows. `pandya_rows`: take the particle-hole rows held by one device: channels q with the same q // 6, rows r with the same r // (2048 // 4). Among them, the rows naming particle-particle channels c with one value of c // 2 number at most 192, and exactly 192 for some value in every such group; those that also name rows p with one value of p // (2048 // 4) number at most 48, and exactly 48 for some values in every such group.
All inputs are finite; a program needn't handle non-finite values.
Results may differ from a plain program's by a relative error of at most 0.0095.
Values may be sent and summed in bfloat16 or wider, within the bound.
A program may use at most 128 MiB of HBM per device.

v0:
```python
import jax
import jax.numpy as jnp
from jax import lax
from jax.sharding import PartitionSpec as P


def place_slots(target, target_count, capacity):
    onehot = (target[:, None] == jnp.arange(target_count, dtype=jnp.int32)[None, :]).astype(
        jnp.int32
    )
    position = jnp.sum(jnp.cumsum(onehot, axis=0) * onehot, axis=1) - 1
    return target * capacity + position


def per_device(
    block_sizes,
    amplitudes,
    ladder_coupling,
    bare_coupling,
    particle_energy,
    hole_energy,
    cycle_coupling,
    pandya_rows,
    pandya_weight,
):
    chan_count = lax.axis_size("chan")
    rep_index = lax.axis_index("rep")
    channels, block_rows, pair_width = amplitudes.shape
    share_rows = ladder_coupling.shape[1]
    ph_share = cycle_coupling.shape[2]
    wanted = pandya_rows.reshape(-1)
    row_count = wanted.shape[0]
    capacity = 2 * row_count // chan_count
    local_total = channels * block_rows
    source = wanted // local_total
    local_row = wanted % local_total
    slot_index = place_slots(source, chan_count, capacity)
    request = jnp.zeros((chan_count * capacity,), jnp.int32).at[slot_index].set(local_row)
    request = request.reshape(chan_count, capacity)
    flat_amp = amplitudes.reshape(local_total, pair_width)
    asked_rows = lax.all_to_all(request, "chan", split_axis=0, concat_axis=0, tiled=True)
    found_rows = flat_amp[asked_rows]
    sent_rows = lax.all_to_all(found_rows, "chan", split_axis=0, concat_axis=0, tiled=True)
    picked = sent_rows.reshape(chan_count * capacity, pair_width)[slot_index]
    weights = pandya_weight.reshape(row_count, 1)
    recoupled = (weights * picked.astype(jnp.float32)).astype(jnp.bfloat16)
    recoupled = recoupled.reshape(pandya_rows.shape + (pair_width,))
    partial_value = lax.dot_general(
        cycle_coupling, recoupled, (((2,), (1,)), ((0,), (0,))), preferred_element_type=jnp.float32
    )
    cycle_whole = lax.psum(partial_value.astype(jnp.bfloat16), "rep").astype(jnp.float32)
    cycle_mine = lax.dynamic_slice_in_dim(cycle_whole, rep_index * ph_share, ph_share, 1)
    returned = (weights * cycle_mine.reshape(row_count, pair_width)).astype(jnp.bfloat16)
    outgoing = (
        jnp.zeros((chan_count * capacity, pair_width), jnp.bfloat16).at[slot_index].set(returned)
    )
    arrived = lax.all_to_all(
        outgoing.reshape(chan_count, capacity, pair_width),
        "chan",
        split_axis=0,
        concat_axis=0,
        tiled=True,
    )
    gathered = (
        jnp.zeros((local_total, pair_width), jnp.float32)
        .at[asked_rows.reshape(-1)]
        .add(arrived.reshape(-1, pair_width).astype(jnp.float32))
    )
    cycle_pairs = lax.psum_scatter(
        gathered.reshape(channels, block_rows, pair_width).astype(jnp.bfloat16),
        "rep",
        scatter_dimension=1,
        tiled=True,
    ).astype(jnp.float32)
    row_ids = jnp.arange(block_rows, dtype=jnp.int32)
    usable = row_ids[None, :] < block_sizes[:, None]
    masked = jnp.where(usable[:, :, None], amplitudes, jnp.zeros_like(amplitudes))
    ladder = lax.dot_general(
        ladder_coupling, masked, (((2,), (1,)), ((0,), (0,))), preferred_element_type=jnp.float32
    )
    own_rows = rep_index * share_rows + jnp.arange(share_rows, dtype=jnp.int32)
    own_valid = own_rows[None, :] < block_sizes[:, None]
    numer = bare_coupling.astype(jnp.float32) + 0.5 * ladder + cycle_pairs
    denom = particle_energy[:, :, None] - hole_energy[:, None, :]
    result = jnp.where(own_valid[:, :, None], numer / denom, jnp.zeros_like(numer))
    return result.astype(jnp.bfloat16)


def solution(mesh):
    in_specs = (
        P("chan"),
        P("chan", None, None),
        P("chan", "rep", None),
        P("chan", "rep", None),
        P("chan", "rep"),
        P("chan", None),
        P("chan", None, "rep"),
        P("chan", "rep"),
        P("chan", "rep"),
    )
    out_specs = P("chan", "rep", None)
    return jax.shard_map(
        per_device, mesh=mesh, in_specs=in_specs, out_specs=out_specs, check_vma=False
    )
```

profile of v0, /device:TPU:1, one launch (start us, length us, event | category | flops | bytes accessed | tf_op | source)
XLA Modules:
  0.0 568.0 jit_solution(7254446725257351599)
XLA Ops:
  6.5 0.0 copy-start
  6.5 0.9 reshape.277
  7.4 1.4 reshape.276
  8.8 0.8 fusion.19
  9.6 16.1 %reduce-window.6 = s32[32,24,128]{2,1,0:T(8,128)S(1)} reduce-window(s32[32,24,128]{2,1,0:T(8,128)} %fusion.19, s32[]{:T(128)} %constant.51.clone.1), window={size=1x1x128 pad=0_0x0_0x127_0}, to_apply=%region_0.1 | reduce-window | flops 12484608 | bytes 786436 | tf_op jit(solution)/shard_map/reduce-window
  25.7 0.9 slice.12
  26.6 1.8 copy.23
  28.5 0.9 reduce-window.9
  29.3 0.2 broadcast_add_fusion
  29.5 0.7 add_select_fusion
  30.2 0.1 fusion.18
  30.4 0.7 copy.24
  31.1 0.1 compare_select_fusion.2
  31.2 11.8 %scatter_custom_fusion = s32[6144]{0:T(1024)S(1)} fusion(s32[3072]{0:T(1024)S(1)} %bitcast.62, s32[3072]{0:T(1024)S(1)} %get-tuple-element.5, s32[]{:T(128)} %constant.51.clone.1), kind=kCustom, calls=%fused_computation.54 | custom fusion | bytes 24580 | tf_op jit(solution)/shard_map/scatter | solution.py:38
  43.0 0.1 all_to_all.14
  43.1 16.5 %all_to_all.22 = s32[32,1,192]{2,1,0:T(1,128)S(1)} all-to-all(s32[32,1,192]{2,1,0:T(1,128)S(1)} %all_to_all.14), channel_id=1, replica_groups=mesh['chan'=32,'rep'=4] {'chan'}, dimensions={0} | all-to-all | bytes 49152 | tf_op jit(solution)/shard_map/all_to_all | solution.py:41
  59.6 0.1 fusion.20
  59.7 0.1 reshape.288
  59.8 0.0 copy-done
  59.8 25.1 %gather_fusion = bf16[6144,384]{1,0:T(8,128)(2,1)} fusion(bf16[4096,384]{1,0:T(8,128)(2,1)S(1)} %bitcast.52, s32[6144]{0:T(1024)S(1)} %broadcast_clamp_fusion), kind=kCustom, calls=%fused_computation | custom fusion | bytes 9461760 | tf_op jit(solution)/shard_map/gather | solution.py:42
  84.9 4.8 all-to-all-start.1
  89.8 0.2 all-reduce.2.cloned.1.call-start
  90.0 58.3 %all-to-all-done.1 = bf16[32,192,384]{2,1,0:T(8,128)(2,1)} async-done(((bf16[32,192,384]{2,1,0:T(8,128)(2,1)}), bf16[32,192,384]{2,1,0:T(8,128)(2,1)}, u32[]{:S(2)}, u32[]{:S(2)}) %all-to-all-start.1) | async-done | bytes 4718624 | tf_op jit(solution)/shard_map/all_to_all | solution.py:43
  148.3 15.7 %gather_fusion.1 = bf16[3072,384]{1,0:T(8,128)(2,1)} fusion(bf16[6144,384]{1,0:T(8,128)(2,1)} %bitcast.10, s32[3072]{0:T(1024)S(1)} %broadcast_clamp_fusion.1), kind=kCustom, calls=%fused_computation.1 | custom fusion | bytes 4730880 | tf_op jit(solution)/shard_map/gather | solution.py:44
  164.0 0.0 copy-start.1
  164.0 4.5 copy.18
  168.6 0.0 copy-done.1
  168.6 15.9 %convert_bitcast_fusion = bf16[6,2048,384]{1,2,0:T(8,128)(2,1)} fusion(bf16[6,2048,512]{2,1,0:T(8,128)(2,1)} %param.15, f32[6,512,384]{1,2,0:T(8,128)} %copy.18, f32[6,512]{1,0:T(8,128)S(1)} %copy-done.1), kind=kOutput, calls=%fused_computation.7 | convolution fusion | flops 4838916096 | bytes 26750976 | tf_op jit(solution)/shard_map/dot_general | solution.py:48
  184.5 0.0 all-reduce.2.cloned.1.call-update
  184.5 178.6 %all-reduce.2.cloned.1.call-done = bf16[6,2048,384]{1,2,0:T(8,128)(2,1)} async-done(((bf16[6,2048,384]{1,2,0:T(8,128)(2,1)}), bf16[6,2048,384]{1,2,0:T(8,128)(2,1)}) %all-reduce.2.cloned.1.call-update) | async-done | bytes 9437200 | tf_op jit(solution)/shard_map/psum | solution.py:51
  363.1 4.6 dynamic-slice_convert_fusion
  367.7 6.0 %copy.19 = f32[6,512,384]{2,1,0:T(8,128)} copy(f32[6,512,384]{1,2,0:T(8,128)} %dynamic-slice_convert_fusion) | data formatting | bytes 9437184 | tf_op jit(solution)/shard_map/dynamic_slice | solution.py:52
  373.7 4.3 fusion.2
  378.0 17.1 %scatter_custom_fusion.1 = bf16[6144,384]{1,0:T(8,128)(2,1)} fusion(s32[3072]{0:T(1024)S(1)} %bitcast.64, bf16[3072,384]{1,0:T(8,128)(2,1)} %fusion.2, bf16[]{:T(256)} %constant.25.clone.1), kind=kCustom, calls=%fused_computation.17 | custom fusion | bytes 4719104 | tf_op jit(solution)/shard_map/scatter | solution.py:55
  395.1 7.7 %all-to-all-start.2 = ((bf16[32,192,384]{2,1,0:T(8,128)(2,1)}), bf16[32,192,384]{2,1,0:T(8,128)(2,1)}, u32[]{:S(2)}, u32[]{:S(2)}) async-start(bf16[32,192,384]{2,1,0:T(8,128)(2,1)} %bitcast.54), calls=%async_computation.2 | async-start | bytes 9437184 | tf_op jit(solution)/shard_map/all_to_all | solution.py:57
  402.8 0.3 reduce-scatter.2.cloned.1.call-start
  403.0 0.1 reduce
  403.1 0.1 reshape.279
  403.3 57.9 %all-to-all-done.2 = bf16[32,192,384]{2,1,0:T(8,128)(2,1)} async-done(((bf16[32,192,384]{2,1,0:T(8,128)(2,1)}), bf16[32,192,384]{2,1,0:T(8,128)(2,1)}, u32[]{:S(2)}, u32[]{:S(2)}) %all-to-all-start.2) | async-done | bytes 4718624 | tf_op jit(solution)/shard_map/all_to_all | solution.py:57
  461.2 43.5 %scatter_custom_fusion.2 = f32[4096,384]{1,0:T(8,128)} fusion(s32[6144]{0:T(1024)S(1)} %bitcast.66, bf16[6144,384]{1,0:T(8,128)(2,1)} %bitcast.18, f32[]{:T(128)} %constant.50.clone.1), kind=kCustom, calls=%fused_computation.5 | custom fusion | flops 4718592 | bytes 11010052 | tf_op jit(solution)/shard_map/scatter-add | solution.py:67
  504.7 4.8 convert_element_type.60
  509.5 0.0 copy-start.2
  509.5 0.0 copy-start.3
  509.5 0.0 copy-start.4
  509.5 4.8 copy.20
  514.3 0.0 reduce-scatter.2.cloned.1.call-update
  514.4 2.3 copy.14
  516.6 0.0 copy-done.2
  516.7 0.1 broadcast_compare_fusion
  516.7 0.1 iota_compare_fusion.2
  516.8 36.1 %reduce-scatter.2.cloned.1.call-done = bf16[2,512,384]{1,2,0:T(8,128)(2,1)} async-done(((bf16[2,2048,384]{1,2,0:T(8,128)(2,1)}), bf16[2,512,384]{1,2,0:T(8,128)(2,1)}) %reduce-scatter.2.cloned.1.call-update) | async-done | bytes 786448 | tf_op jit(solution)/shard_map/reduce_scatter | solution.py:69
  552.9 0.0 copy-done.3
  552.9 0.0 copy-done.4
  552.9 5.9 %fusion.14 = bf16[2,512,384]{1,2,0:T(8,128)(2,1)} fusion(bf16[2,512,384]{1,2,0:T(8,128)(2,1)} %reduce-scatter.2.cloned.1.call-done, bf16[2,512,384]{1,2,0:T(8,128)(2,1)} %copy.14, f32[2,384]{1,0:T(2,128)S(1)} %copy-done.4, f32[2,512]{1,0:T(2,128)S(1)} %copy-done.3, pred[2,512]{1,0:T(4,128)(4,1)S(1)} %broadcast_compare_fusion, ...), kind=kOutput, calls=%fused_computation.24 | convolution fusion | flops 1615724544 | bytes 9711616 | tf_op jit(solution)/shard_map/dot_general | solution.py:78
  558.9 2.3 copy.21
  (7 shorter events, 0.1 us)
Async XLA Ops:
  6.5 53.3 %copy-start = (bf16[2,2048,384]{2,1,0:T(8,128)(2,1)S(1)}, bf16[2,2048,384]{2,1,0:T(8,128)(2,1)}, u32[]{:S(2)}) copy-start(bf16[2,2048,384]{2,1,0:T(8,128)(2,1)} %param.10) | copy-start | bytes 9437188
  84.9 63.4 %all-to-all-start.1 = ((bf16[32,192,384]{2,1,0:T(8,128)(2,1)}), bf16[32,192,384]{2,1,0:T(8,128)(2,1)}, u32[]{:S(2)}, u32[]{:S(2)}) async-start(bf16[32,192,384]{2,1,0:T(8,128)(2,1)} %bitcast.53), calls=%async_computation.1 | async-start | bytes 9437184 | tf_op jit(solution)/shard_map/all_to_all | solution.py:43
  89.8 273.4 %all-reduce.2.cloned.1.call-start = ((), (), s32[]{:S(2)}) async-start(), calls=%async_computation.4 | async-start | bytes 18874368 | tf_op jit(solution)/shard_map/psum | solution.py:51
  164.0 4.5 copy-start.1
  395.1 66.1 %all-to-all-start.2 = ((bf16[32,192,384]{2,1,0:T(8,128)(2,1)}), bf16[32,192,384]{2,1,0:T(8,128)(2,1)}, u32[]{:S(2)}, u32[]{:S(2)}) async-start(bf16[32,192,384]{2,1,0:T(8,128)(2,1)} %bitcast.54), calls=%async_computation.2 | async-start | bytes 9437184 | tf_op jit(solution)/shard_map/all_to_all | solution.py:57
  402.8 150.1 %reduce-scatter.2.cloned.1.call-start = ((), (), s32[]{:S(2)}) async-start(), calls=%async_computation.5 | async-start | bytes 3932160 | tf_op jit(solution)/shard_map/reduce_scatter | solution.py:69
  509.5 7.1 %copy-start.2 = (s32[2]{0:T(128)S(1)}, s32[2]{0:T(128)}, u32[]{:S(2)}) copy-start(s32[2]{0:T(128)} %param.9) | copy-start | bytes 28
  509.5 43.4 %copy-start.3 = (f32[2,512]{1,0:T(2,128)S(1)}, f32[2,512]{1,0:T(2,128)}, u32[]{:S(2)}) copy-start(f32[2,512]{1,0:T(2,128)} %param.13) | copy-start | bytes 12292
  509.5 43.4 %copy-start.4 = (f32[2,384]{1,0:T(2,128)S(1)}, f32[2,384]{1,0:T(2,128)}, u32[]{:S(2)}) copy-start(f32[2,384]{1,0:T(2,128)} %param.14) | copy-start | bytes 9220
Sparse Core Ops, SparseCore 0:
  184.6 178.4 all-reduce.1
  514.5 38.3 reduce-scatter.1
where the time goes:
time: 570 us; the launch traced here: 568 us
  waiting for transfers between devices  331 us (58%)
  local copies, waits for them, and re-layouts  95.7 us (17%)
  other arithmetic  76.4 us (13%)
  matrix products  21.9 us (4%)
  blocking collectives  16.5 us (3%)
  between operations  13.5 us (2%)
  starting transfers between devices  13 us (2%)
    psum x1, waiting for transfers between devices, per_device(): lax.psum(partial_value.astype(jnp.bfloat16), 'rep').astype(jnp.float32)  179 us
    all_to_all x1, waiting for transfers between devices, per_device(): lax.all_to_all(found_rows, 'chan', split_axis=0, concat_axis=0, tiled=True)  58.3 us
    all_to_all x1, waiting for transfers between devices, per_device(): lax.all_to_all(outgoing.reshape(chan_count, capacity, pair_width), 'chan'...  57.9 us
    scatter-add x1, other arithmetic, per_device(): gathered = jnp.zeros((local_total, pair_width), jnp.float32).at[asked_row...  43.5 us
    reduce_scatter x1, waiting for transfers between devices, per_device(): lax.psum_scatter(gathered.reshape(channels, block_rows, pair_width).astyp...  36.1 us
    gather x1, local copies, waits for them, and re-layouts, per_device(): found_rows = flat_amp[asked_rows]  25.1 us
    another operation x3, other arithmetic  17.2 us
    scatter x1, local copies, waits for them, and re-layouts, per_device(): jnp.zeros((chan_count * capacity, pair_width), jnp.bfloat16).at[slot_index]  17.1 us
  transfers between devices with their start and end apart: 4, of which 4 were waited for; matrix products, arithmetic and copies ran while one was open for 0% of the time, Pallas kernels for 0%

commit v1 on v0

v1 whole, which is shorter than its diff:
```python
import functools

import jax
import jax.numpy as jnp
from jax import lax
from jax.experimental import pallas as pl
from jax.experimental.pallas import tpu as pltpu
from jax.sharding import PartitionSpec as P

MESH = pl.DeviceIdType.MESH
BF = jnp.bfloat16
F32 = jnp.float32
I32 = jnp.int32

CHUNKS = ((0, 128), (128, 256))
CAP = 48
NT = (((1,), (1,)), ((), ()))


def dot(a, b):
    return jnp.dot(a, b, preferred_element_type=F32)


def iota(shape, dim):
    return lax.broadcasted_iota(I32, shape, dim)


def one_hot(mask):
    return jnp.where(mask, 1.0, 0.0).astype(BF)


def prep_kernel(rows_ref, weight_ref, energy_ref, slot_ref, back_ref, req_ref, cols_ref):
    blocks, width = rows_ref.shape
    upper = one_hot(iota((width, width), 0) <= iota((width, width), 1))
    key_ids = iota((256, width), 0)
    carry = jnp.zeros((256, 1), F32)
    tables = jnp.zeros((1024, 128), F32)
    for q in range(blocks):
        g = rows_ref[q : q + 1, :]
        chan = g >> 12
        quarter = (g >> 9) & 3
        inner = ((g >> 11) & 1) * 512 + (g & 511) + 1
        number = q * width + iota((1, width), 1) + 1
        hit = jnp.where(key_ids == chan * 8 + quarter, 1.0, 0.0)
        count = dot(hit.astype(BF), upper) + carry
        place = (jnp.sum(hit * count, axis=0, keepdims=True) - 1.0).astype(I32)
        carry = carry + jnp.sum(hit, axis=1, keepdims=True)
        at = one_hot(iota((128, width), 0) == place)
        parts = (inner >> 5, inner & 31, number >> 6, number & 63)
        values = jnp.concatenate([(hit * p.astype(F32)).astype(BF) for p in parts], axis=0)
        tables = tables + lax.dot_general(values, at, NT, preferred_element_type=F32)
        slot_ref[q : q + 1, :] = chan * (4 * CAP) + quarter * CAP + place
    req_ref[...] = (tables[0:256] * 32.0 + tables[256:512] - 1.0).astype(I32)
    back_ref[...] = jnp.maximum(tables[512:768] * 64.0 + tables[768:1024] - 1.0, 0.0).astype(I32)
    lanes = [weight_ref[q : q + 1, b * 128 : (b + 1) * 128] for q in range(blocks) for b in range(4)]
    lanes += [energy_ref[c : c + 1, b * 128 : (b + 1) * 128] for c in range(2) for b in range(4)]
    lanes.append(jnp.zeros((128 - len(lanes), 128), F32))
    cols_ref[...] = jnp.concatenate(lanes, axis=0).T


def prepare(rows, weight, energy):
    vmem = pl.BlockSpec(memory_space=pltpu.VMEM)
    return pl.pallas_call(
        prep_kernel,
        out_shape=(
            jax.ShapeDtypeStruct(rows.shape, I32),
            jax.ShapeDtypeStruct((256, 128), I32),
            jax.ShapeDtypeStruct((256, 128), I32),
            jax.ShapeDtypeStruct((128, 128), F32),
        ),
        in_specs=[vmem] * 3,
        out_specs=(vmem,) * 4,
    )(rows, weight, energy)


def main_kernel(
    slot_ref, back_ref, sizes_ref, req_ref, cols_ref, hole_ref, spread_ref, owner_ref, ownert_ref,
    amp_hbm, ladder_hbm, bare_hbm, cycle_hbm, out_ref,
    amp, bare, cyc, asked, mine, theirs, ordered, col, hot, x, rq, rec, stage, acc,
    *rest,
):
    n = len(CHUNKS)
    fs, fr, part, two, raw, comb, rv = (rest[i * n : (i + 1) * n] for i in range(7))
    (in_sem, cyc_sem, req_ss, req_rs, tab_ss, tab_rs,
     fwd_ss, fwd_rs, rs_ss, rs_rs, ret_ss, ret_rs) = rest[7 * n :]

    me = lax.axis_index("chan")
    my = lax.axis_index("rep")
    mx, mz, mc = lax.div(me, 8), lax.rem(lax.div(me, 2), 4), lax.rem(me, 2)

    def chan_of(dx, dz, dc, sign=1):
        xx = lax.rem(mx + sign * dx + 4, 4)
        zz = lax.rem(mz + sign * dz + 4, 4)
        return (xx * 4 + zz) * 2 + lax.rem(mc + dc, 2)

    def plane_peer(t):
        s = lax.rem(t * 13, 32)
        return chan_of(lax.rem(lax.div(s, 2), 4), lax.div(s, 8), lax.rem(s, 2))

    def cube_peer(t, sign=1):
        s = lax.rem(t * 45, 128)
        chan = chan_of(lax.rem(lax.div(s, 2), 4), lax.rem(lax.div(s, 8), 4), lax.rem(s, 2), sign)
        return chan, lax.rem(my + sign * lax.div(s, 32) + 4, 4)

    def rep_peer(d):
        return lax.rem(my + d, 4)

    def remote(src, dst, ss, rs, chan=None, rep=None):
        device = {}
        if chan is not None:
            device["chan"] = chan
        if rep is not None:
            device["rep"] = rep
        return pltpu.make_async_remote_copy(src, dst, ss, rs, device_id=device, device_id_type=MESH)

    amp_cp = pltpu.make_async_copy(amp_hbm, amp, in_sem.at[0])
    bare_cp = pltpu.make_async_copy(bare_hbm, bare, in_sem.at[1])
    amp_cp.start()
    bare_cp.start()
    lad_cps = [
        pltpu.make_async_copy(
            ladder_hbm.at[c, :, pl.ds(k * 512, 512)], cyc.at[c, pl.ds(k * 512, 512)], in_sem.at[2 + 4 * c + k]
        )
        for c in range(2)
        for k in range(4)
    ]
    for cp in lad_cps:
        cp.start()

    def cyc_copy(i):
        return pltpu.make_async_copy(cycle_hbm.at[i % 6], cyc.at[(i + 2) % 3], cyc_sem.at[(i + 2) % 3])

    cyc_copy(0).start()

    barrier = pltpu.get_barrier_semaphore()

    @pl.loop(1, 128)
    def _(t):
        chan, rep = cube_peer(t)
        pl.semaphore_signal(barrier, inc=1, device_id={"chan": chan, "rep": rep}, device_id_type=MESH)

    pl.semaphore_wait(barrier, 127)

    @pl.loop(1, 32)
    def _(t):
        p = plane_peer(t)
        remote(req_ref.at[p], asked.at[me], req_ss, req_rs, chan=p).start()

    asked[me] = req_ref[me]
    req_all = remote(req_ref.at[pl.ds(0, 31)], asked.at[pl.ds(0, 31)], req_ss, req_rs, chan=plane_peer(1))
    req_all.wait_recv()

    for q in range(4):
        mine[q] = asked[:, q, :]
    tab_cps = []
    for d in range(1, 4):
        to = rep_peer(d)
        cp = remote(mine.at[to], theirs.at[my], tab_ss.at[d - 1], tab_rs.at[d - 1], rep=to)
        cp.start()
        tab_cps.append(cp)
    theirs[my] = mine[my]

    def table_parts(table):
        t = table + 1
        return (t >> 5).astype(F32).astype(BF), (t & 31).astype(F32).astype(BF)

    for q in range(4):
        hi, lo = table_parts(mine[q])
        for b in range(4):
            rows = pl.ds(b * 384, 384)
            spread = spread_ref[rows, :]
            found = lax.dot_general(spread, hi, NT, preferred_element_type=F32) * 32.0
            found = found + lax.dot_general(spread, lo, NT, preferred_element_type=F32)
            found = jnp.sum(found * owner_ref[rows, :], axis=1, keepdims=True) - 1.0
            col[q, rows, :] = jnp.broadcast_to(found, (384, 128)).astype(I32)

    amp_cp.wait()

    def gather(k):
        c0, w = CHUNKS[k]

        @pl.loop(0, 4)
        def _(g):
            for q in range(4):
                for u in range(8):
                    p = plane_peer(g * 8 + u)
                    want = col[q, pl.ds(pl.multiple_of(p * CAP, CAP), CAP), :]
                    for b in range(8):
                        lane = iota((CAP, 128), 1) + b * 128
                        hot[u * CAP : (u + 1) * CAP, b * 128 : (b + 1) * 128] = one_hot(want == lane)
                got = dot(hot[:, 0:512], amp[0, q * 512 : (q + 1) * 512, c0 : c0 + w])
                got = got + dot(hot[:, 512:1024], amp[1, q * 512 : (q + 1) * 512, c0 : c0 + w])
                got = got.astype(BF)
                for u in range(8):
                    p = plane_peer(g * 8 + u)
                    fs[k][p, q * CAP : (q + 1) * CAP, :] = got[u * CAP : (u + 1) * CAP]

            for u in range(8):
                p = plane_peer(g * 8 + u)
                if u == 0:

                    @pl.when(g > 0)
                    def _():
                        remote(fs[k].at[p], fr[k].at[me], fwd_ss.at[k], fwd_rs.at[k], chan=p).start()
                else:
                    remote(fs[k].at[p], fr[k].at[me], fwd_ss.at[k], fwd_rs.at[k], chan=p).start()

        fr[k][me] = fs[k][me]

    for k in range(n):
        gather(k)

    bare_cp.wait()
    for c in range(2):
        for k in range(4):
            lad_cps[4 * c + k].wait()
        for k in range(4):
            usable = iota((512, 384), 0) + k * 512 < sizes_ref[c]
            block = amp[c, k * 512 : (k + 1) * 512, :].astype(F32)
            masked = jnp.where(usable, block, 0.0).astype(BF)
            term = 0.5 * dot(cyc[c, k * 512 : (k + 1) * 512, :], masked)
            if k == 0:
                acc[c * 512 : (c + 1) * 512, :] = bare[c].astype(F32) + term
            else:
                acc[c * 512 : (c + 1) * 512, :] += term
    cyc_copy(1).start()
    cyc_copy(2).start()

    for cp in tab_cps:
        cp.wait_recv()

    @pl.loop(0, 128)
    def _(t):
        chan, rep = cube_peer(t, -1)
        ordered[pl.ds(t, 1), :] = theirs[rep, pl.ds(chan, 1), :]

    def rs_copy(k, q, i):
        up, down = rep_peer(1), rep_peer(3)
        far = rep_peer(2) * 512
        rows = lambda start: part[k].at[q, pl.ds(pl.multiple_of(start, 256), 256)]
        args = (
            (rows(far), two[k].at[0, q], up),
            (rows(far + 256), two[k].at[1, q], down),
            (rows(up * 512 + 256), raw[k].at[0, q], up),
            (rows(down * 512), raw[k].at[1, q], down),
            (rows(up * 512), comb[k].at[0, q], up),
            (rows(down * 512 + 256), comb[k].at[1, q], down),
        )
        src, dst, to = args[i]
        return remote(src, dst, rs_ss.at[k, q, i], rs_rs.at[k, q, i], rep=to)

    def forward(k):
        c0, w = CHUNKS[k]
        done = remote(fs[k].at[pl.ds(0, 31)], fr[k].at[pl.ds(0, 31)], fwd_ss.at[k], fwd_rs.at[k], chan=plane_peer(1))
        done.wait_recv()
        done.wait_send()

        @pl.loop(0, 32)
        def _(s):
            for v in range(w // 128):
                x[v, pl.ds(pl.multiple_of(s * 192, 192), 192), :] = (
                    fr[k][s, :, v * 128 : (v + 1) * 128].astype(F32)
                )

        for q in range(6):

            @pl.loop(0, 32)
            def _(i):
                for u in range(16):
                    r = i * 16 + u
                    slot = slot_ref[q, r]
                    for v in range(w // 128):
                        rq[v, pl.ds(r, 1), :] = x[v, pl.ds(slot, 1), :]

            for b in range(4):
                rows = slice(b * 128, (b + 1) * 128)
                scale = jnp.broadcast_to(cols_ref[:, q * 4 + b : q * 4 + b + 1], (128, 128))
                for v in range(w // 128):
                    rec[rows, v * 128 : (v + 1) * 128] = (rq[v, rows, :] * scale).astype(BF)
            right = rec[:, 0:w]
            i = k * 6 + q
            cyc_copy(i).wait()
            for b in range(4):
                rows = slice(b * 512, (b + 1) * 512)
                part[k][q, rows, :] = dot(cyc[(i + 2) % 3, rows, :], right).astype(BF)
            if i + 3 < 6 * n:
                cyc_copy(i + 3).start()
            for j in range(4):
                rs_copy(k, q, j).start()
            if q >= 1:
                relay(k, q - 1)
        relay(k, 5)

    def relay(k, q):
        for j, start in ((0, rep_peer(1) * 512), (1, rep_peer(3) * 512 + 256)):
            rs_copy(k, q, j).wait_recv()
            rows = pl.ds(pl.multiple_of(start, 256), 256)
            part[k][q, rows, :] = (part[k][q, rows, :].astype(F32) + two[k][j, q].astype(F32)).astype(BF)
            rs_copy(k, q, 4 + j).start()

    def back(k):
        c0, w = CHUNKS[k]
        for q in range(6):
            for j in range(2, 6):
                rs_copy(k, q, j).wait_recv()
            for j in range(6):
                rs_copy(k, q, j).wait_send()
            for b in range(4):
                rows = pl.ds(pl.multiple_of(my * 512 + b * 128, 128), 128)
                half = slice((b % 2) * 128, (b % 2) * 128 + 128)
                if b < 2:
                    other = comb[k][0, q, half, :].astype(F32) + raw[k][1, q, half, :].astype(F32)
                else:
                    other = raw[k][0, q, half, :].astype(F32) + comb[k][1, q, half, :].astype(F32)
                total = part[k][q, rows, :].astype(F32) + other
                total = total * cols_ref[:, q * 4 + b : q * 4 + b + 1]
                for v in range(w // 128):
                    x[v, q * 512 + b * 128 : q * 512 + (b + 1) * 128, :] = total[:, v * 128 : (v + 1) * 128]

        def fill(t):
            chan, rep = cube_peer(t)
            key = chan * 8 + rep
            for j in range(CAP):
                row = back_ref[key, j]
                for v in range(w // 128):
                    stage[v, j : j + 1, :] = x[v, pl.ds(row, 1), :]
            rows = jnp.concatenate([stage[v] for v in range(w // 128)], axis=1)
            return chan, rep, rows.astype(BF)

        send = fs[k]
        chan, rep, rows = fill(0)
        rv[k][0] = rows

        @pl.loop(1, 128)
        def _(t):
            chan, rep, rows = fill(t)
            place = (lax.div(t, 4), pl.ds(pl.multiple_of(lax.rem(t, 4) * CAP, CAP), CAP))
            send[place[0], place[1], :] = rows
            remote(
                send.at[place[0], place[1]], rv[k].at[t], ret_ss.at[k], ret_rs.at[k, lax.div(t, 16)],
                chan=chan, rep=rep,
            ).start()

    def collect(k):
        c0, w = CHUNKS[k]
        for ph in range(8):
            first = 1 if ph == 0 else 0
            src = rv[k].at[pl.ds(ph * 16 + first, 16 - first)]
            chan, rep = cube_peer(1)
            remote(src, src, ret_ss.at[k], ret_rs.at[k, ph], chan=chan, rep=rep).wait_recv()
            hi, lo = table_parts(ordered[ph * 16 : (ph + 1) * 16, :])
            spread = spread_ref[0:768, :]
            found = lax.dot_general(hi, spread, NT, preferred_element_type=F32) * 32.0
            found = found + lax.dot_general(lo, spread, NT, preferred_element_type=F32)
            found = (jnp.sum(found * ownert_ref[...], axis=0, keepdims=True) - 1.0).astype(I32)
            rows = rv[k][ph * 16 : (ph + 1) * 16].reshape(16 * CAP, w)
            for b in range(4):
                at = one_hot(iota((256, 16 * CAP), 0) + b * 256 == found)
                acc[b * 256 : (b + 1) * 256, c0 : c0 + w] += dot(at, rows)
        for c in range(2):
            for b in range(4):
                rows = slice(c * 512 + b * 128, c * 512 + (b + 1) * 128)
                pe = cols_ref[:, 24 + c * 4 + b : 25 + c * 4 + b]
                value = acc[rows, c0 : c0 + w] / (pe - hole_ref[c : c + 1, c0 : c0 + w])
                usable = my * 512 + b * 128 + iota((128, w), 0) < sizes_ref[c]
                out_ref[c, b * 128 : (b + 1) * 128, c0 : c0 + w] = jnp.where(usable, value, 0.0).astype(BF)

    for k in range(n):
        forward(k)
        back(k)
    for k in range(n):
        collect(k)

    req_all.wait_send()
    for cp in tab_cps:
        cp.wait_send()
    chan, rep = cube_peer(1)
    for k in range(n):
        src = rv[k].at[pl.ds(0, 127)]
        remote(src, src, ret_ss.at[k], ret_rs.at[k, 0], chan=chan, rep=rep).wait_send()


def per_device(
    block_sizes, amplitudes, ladder_coupling, bare_coupling, particle_energy, hole_energy,
    cycle_coupling, pandya_rows, pandya_weight,
):
    slots, back, requests, cols = prepare(pandya_rows, pandya_weight, particle_energy)
    ids = jnp.arange(32 * CAP, dtype=I32)[:, None]
    lane = jnp.arange(128, dtype=I32)[None, :]
    spread = (ids % CAP == lane).astype(BF)
    owner = (ids // CAP == lane[:, :32]).astype(F32)
    ownert = (jnp.arange(16 * CAP, dtype=I32)[None, :] // CAP == jnp.arange(16, dtype=I32)[:, None]).astype(F32)
    vmem = pl.BlockSpec(memory_space=pltpu.VMEM)
    smem = pl.BlockSpec(memory_space=pltpu.SMEM)
    hbm = pl.BlockSpec(memory_space=pl.ANY)
    n = len(CHUNKS)
    ws = [w for _, w in CHUNKS]
    wide = max(ws)
    scratch = [
        pltpu.VMEM(amplitudes.shape, BF),
        pltpu.VMEM(bare_coupling.shape, BF),
        pltpu.VMEM((3, 2048, 512), BF),
        pltpu.VMEM((32, 8, 128), I32),
        pltpu.VMEM((4, 32, 128), I32),
        pltpu.VMEM((4, 32, 128), I32),
        pltpu.VMEM((128, 128), I32),
        pltpu.VMEM((4, 32 * CAP, 128), I32),
        pltpu.VMEM((8 * CAP, 1024), BF),
        pltpu.VMEM((wide // 128, 128 * CAP, 128), F32),
        pltpu.VMEM((wide // 128, 512, 128), F32),
        pltpu.VMEM((512, wide), BF),
        pltpu.VMEM((wide // 128, CAP, 128), F32),
        pltpu.VMEM((1024, 384), F32),
    ]
    scratch += [pltpu.VMEM((32, 4 * CAP, w), BF) for w in ws]
    scratch += [pltpu.VMEM((32, 4 * CAP, w), BF) for w in ws]
    scratch += [pltpu.VMEM((6, 2048, w), BF) for w in ws]
    for _ in range(3):
        scratch += [pltpu.VMEM((2, 6, 256, w), BF) for w in ws]
    scratch += [pltpu.VMEM((128, CAP, w), BF) for w in ws]
    sem = pltpu.SemaphoreType.DMA
    scratch += [
        sem((10,)), sem((3,)), sem, sem, sem((3,)), sem((3,)),
        sem((n,)), sem((n,)), sem((n, 6, 6)), sem((n, 6, 6)), sem((n,)), sem((n, 8)),
    ]
    return pl.pallas_call(
        main_kernel,
        out_shape=jax.ShapeDtypeStruct(bare_coupling.shape, BF),
        in_specs=[smem] * 3 + [vmem] * 6 + [hbm] * 4,
        out_specs=vmem,
        scratch_shapes=scratch,
        compiler_params=pltpu.CompilerParams(
            collective_id=0, has_side_effects=True, vmem_limit_bytes=60 * 1024 * 1024
        ),
        cost_estimate=pl.CostEstimate(flops=20_000_000_000, bytes_accessed=40_000_000, transcendentals=0),
    )(
        slots, back, block_sizes, requests.reshape(32, 8, 128), cols, hole_energy, spread, owner, ownert,
        amplitudes, ladder_coupling, bare_coupling, cycle_coupling,
    )


def solution(mesh):
    in_specs = (
        P("chan"),
        P("chan", None, None),
        P("chan", "rep", None),
        P("chan", "rep", None),
        P("chan", "rep"),
        P("chan", None),
        P("chan", None, "rep"),
        P("chan", "rep"),
        P("chan", "rep"),
    )
    out_specs = P("chan", "rep", None)
    return jax.shard_map(
        per_device, mesh=mesh, in_specs=in_specs, out_specs=out_specs, check_vma=False
    )
```

time: 570 us -> 201 us (0.35)
  waiting for transfers between devices: 331 us -> 0 us
  Pallas kernels: 0 us -> 195 us
  local copies, waits for them, and re-layouts: 95.7 us -> 2.1 us
  other arithmetic: 76.4 us -> 2.81 us
  matrix products: 21.9 us -> 0 us
  blocking collectives: 16.5 us -> 0 us
  between operations: 13.5 us -> 0.02 us
  starting transfers between devices: 13 us -> 0 us
    pallas_call x0 -> x2, Pallas kernels: none -> 195 us  [the longest x1 190 us: per_device(): pl.pallas_call(main_kernel, out_shape=jax.ShapeDtypeStruct(bare_coupling....]
    psum x1 -> x0, waiting for transfers between devices: 179 us -> none  [per_device(): lax.psum(partial_value.astype(jnp.bfloat16), 'rep').astype(jnp.float32)]
    all_to_all x2 -> x0, waiting for transfers between devices: 116 us -> none  [the longest x1 58.3 us: per_device(): lax.all_to_all(found_rows, 'chan', split_axis=0, concat_axis=0, tiled=True)]
    scatter-add x1 -> x0, other arithmetic: 43.5 us -> none  [per_device(): gathered = jnp.zeros((local_total, pair_width), jnp.float32).at[asked_row...]
    gather x2 -> x0, local copies, waits for them, and re-layouts: 40.9 us -> none  [the longest x1 25.1 us: per_device(): found_rows = flat_amp[asked_rows]]
    reduce_scatter x1 -> x0, waiting for transfers between devices: 36.1 us -> none  [per_device(): lax.psum_scatter(gathered.reshape(channels, block_rows, pair_width).astyp...]
    scatter x2 -> x0, local copies, waits for them, and re-layouts: 28.9 us -> none  [the longest x1 17.1 us: per_device(): jnp.zeros((chan_count * capacity, pair_width), jnp.bfloat16).at[slot_index]]
    dot_general x2 -> x0, matrix products: 21.9 us -> none  [the longest x1 15.9 us: per_device(): lax.dot_general(cycle_coupling, recoupled, (((2,), (1,)), ((0,), (0,))),...]
  transfers between devices with their start and end apart: 4 -> 0, of which waited for: 4 -> 0; matrix products, arithmetic and copies ran while one was open for 0% -> 0% of each run, Pallas kernels for 0% -> 0%
where the time goes in v1:
time: 201 us; the launch traced here: 200 us
  Pallas kernels  195 us (97%)
  other arithmetic  2.81 us (1%)
  local copies, waits for them, and re-layouts  2.1 us (1%)
    pallas_call x1, Pallas kernels, per_device(): pl.pallas_call(main_kernel, out_shape=jax.ShapeDtypeStruct(bare_coupling....  190 us
    pallas_call x1, Pallas kernels, prepare(): pl.pallas_call(prep_kernel, out_shape=(jax.ShapeDtypeStruct(rows.shape, I...  5.94 us

profile of v1, /device:TPU:1, one launch (start us, length us, event | category | flops | bytes accessed | tf_op | source)
XLA Modules:
  0.0 200.4 jit_solution(13973166798756727154)
XLA Ops:
  0.0 0.6 fusion.1.ownert_ref
  0.7 5.9 %shard_map.91 = (s32[6,512]{1,0:T(8,128)}, s32[256,128]{1,0:T(8,128)}, s32[256,128]{1,0:T(8,128)}, f32[128,128]{1,0:T(8,128)}) custom-call(s32[6,512]{1,0:T(8,128)} %rows_ref.1, f32[6,512]{1,0:T(8,128)} %weight_ref.1, f32[2,512]{1,0:T(2,128)} %energy_ref.1), custom_call_target="tpu_custom_call" | custom-call | tf_op jit(solution)/shard_map/pallas_call | solution.py:63
  6.6 1.0 fusion.spread_ref
  7.6 1.1 compare_convert_fusion.owner_ref
  8.8 189.5 %shard_map.92 = bf16[2,512,384]{2,1,0:T(8,128)(2,1)} custom-call(s32[6,512]{1,0:T(8,128)} %get-tuple-element.9.slot_ref, s32[256,128]{1,0:T(8,128)} %get-tuple-element.10.back_ref, s32[2]{0:T(128)} %sizes_ref.1, s32[32,8,128]{2,1,0:T(8,128)} %bitcast.3, f32[128,128]{1,0:T(8,128)} %get-tuple-element.12.cols_ref, f32[2,384]{1,0:T(2,128)} %hole_ref.1, ...), custom_call_target="tpu_custom_call" | custom-call | flops 20000000000 | bytes 40000000 | tf_op jit(solution)/shard_map/pallas_call | solution.py:426
  198.3 2.1 %copy.12 = bf16[2,512,384]{2,1,0:T(8,128)(2,1)} copy(bf16[2,512,384]{2,1,0:T(8,128)(2,1)} %shard_map.92) | data formatting | bytes 1572864
  (5 shorter events, 0.0 us)
